TPU v7x, 32 devices: a whole 2x2x4 slice. The times are simulated.
32 devices in a mesh: band: 8 (over y, x, core), lev: 4 (over z).
Axes of the slice: x: 2, y: 2, z: 4, core: 2. Of those that a mesh axis runs over, the one named last changes fastest.
Arguments:
- columns: bfloat16 [128, 48, 192, 128], P('band', 'lev'), may hold values from -6 to 6
- vertical: bfloat16 [64, 64], replicated
- row_len: int32 [128], P('band'), may hold values from 20 to 5136, as said below
- wave_order: int32 [1280], replicated, may hold values from 0 to 1279, each once
- legendre: bfloat16 [1280, 128, 1280], P('band'), may hold values from -0.5 to 0.5
Outputs:
- spectra: bfloat16 [1280, 2, 192, 1280], P('band', None, 'lev')
Inputs may be any that keep to these rules, and one draw needn't show every extreme that they name: `row_len`: row lengths are 4 i + 16 for latitude indices i that rise strictly from row to row; the last row is the longest. `wave_order`: each wavenumber appears once.
All inputs are finite; a program needn't handle non-finite values.
Results may differ from a plain program's by a relative error of at most 0.0062.
Values may be sent and summed in bfloat16 or wider, within the bound.
A program may use at most 320 MiB of HBM per device.

v0:
```python
import jax
import jax.numpy as jnp
from jax import lax
from jax.sharding import PartitionSpec as P


def fourier_table(wave_list, length, first_point, points):
    block_count = points // 128
    block_start = first_point + 128 * jnp.arange(block_count, dtype=jnp.int32)
    inner = jnp.arange(128, dtype=jnp.int32)
    step_angle = 6.283185307179586 / length.astype(jnp.float32)
    outer_angle = (block_start[:, None] * wave_list[None, :] % length).astype(
        jnp.float32
    ) * step_angle
    inner_angle = (inner[:, None] * wave_list[None, :] % length).astype(jnp.float32) * step_angle
    outer_cos = jnp.cos(outer_angle)[:, None, :]
    outer_sin = jnp.sin(outer_angle)[:, None, :]
    inner_cos = jnp.cos(inner_angle)[None, :, :]
    inner_sin = jnp.sin(inner_angle)[None, :, :]
    cosine = (outer_cos * inner_cos - outer_sin * inner_sin).reshape(points, -1)
    minus_sine = (-(outer_sin * inner_cos + outer_cos * inner_sin)).reshape(points, -1)
    positions = first_point + jnp.arange(points, dtype=jnp.int32)
    inside = (positions < length)[:, None]
    cosine = jnp.where(inside, cosine, 0.0)
    minus_sine = jnp.where(inside, minus_sine, 0.0)
    return jnp.stack([cosine, minus_sine], axis=1).astype(jnp.bfloat16)


def row_tables(wave_list, lengths, first_point, points):
    return jax.vmap(fourier_table, in_axes=(None, 0, None, None))(
        wave_list, lengths, first_point, points
    )


def per_device(columns, vertical, row_len, wave_order, legendre):
    rows_here, blocks_here, channels, block_width = columns.shape
    levels = vertical.shape[0]
    wave_count = wave_order.shape[0]
    band_count = lax.axis_size("band")
    lev_count = lax.axis_size("lev")
    slots_here = legendre.shape[0]
    shaped = columns.reshape(rows_here, blocks_here, channels // levels, levels, block_width)
    lifted = jnp.einsum("ml,rbflp->rbfmp", vertical, shaped, preferred_element_type=jnp.float32)
    lifted = lifted.astype(jnp.bfloat16).reshape(rows_here, blocks_here, channels, block_width)
    sector_span = blocks_here * block_width
    gathered = lax.all_to_all(lifted, "lev", split_axis=0, concat_axis=1, tiled=True)
    my_rows = gathered.shape[0]
    total_blocks = gathered.shape[1]
    my_lengths = lax.dynamic_slice_in_dim(row_len, lax.axis_index("lev") * my_rows, my_rows)

    def add_group(group_index, running):
        group_piece = lax.dynamic_slice_in_dim(gathered, group_index * blocks_here, blocks_here, 1)
        fourier = row_tables(wave_order, my_lengths, group_index * sector_span, sector_span)
        fourier = fourier.reshape(my_rows, blocks_here, block_width, 2, wave_count)
        return running + jnp.einsum(
            "rbcp,rbpqs->crqs", group_piece, fourier, preferred_element_type=jnp.float32
        )

    initial = jnp.zeros((channels, my_rows, 2, wave_count), jnp.float32)
    group_count = total_blocks // blocks_here
    summed = lax.fori_loop(0, group_count, add_group, initial)
    norm_factor = lax.rsqrt(my_lengths.astype(jnp.float32))
    coeffs = (summed * norm_factor[None, :, None, None]).astype(jnp.bfloat16)
    chan_share = channels // lev_count
    arranged = coeffs.reshape(lev_count, chan_share, my_rows, 2, band_count, slots_here)
    arranged = jnp.transpose(arranged, (1, 2, 3, 4, 0, 5))
    arranged = arranged.reshape(chan_share, my_rows, 2, band_count * lev_count * slots_here)
    owned = lax.all_to_all(arranged, ("band", "lev"), split_axis=3, concat_axis=1, tiled=True)
    own_waves = lax.dynamic_slice_in_dim(
        wave_order, lax.axis_index("band") * slots_here, slots_here
    )
    spectra = jnp.einsum("crqs,srn->sqcn", owned, legendre, preferred_element_type=jnp.float32)
    upper_part = jnp.arange(wave_count, dtype=jnp.int32)[None, :] >= own_waves[:, None]
    return jnp.where(upper_part[:, None, None, :], spectra, 0.0).astype(jnp.bfloat16)


def solution(mesh):
    return jax.shard_map(
        per_device,
        mesh=mesh,
        in_specs=(P("band", "lev", None, None), P(), P("band"), P(), P("band", None, None)),
        out_specs=P("band", None, "lev", None),
        check_vma=False,
    )
```

profile of v0, /device:TPU:0, one launch (start us, length us, event | category | flops | bytes accessed | tf_op | source)
XLA Modules:
  0.0 802.9 jit_solution(5799243325337200030)
XLA Ops:
  0.0 0.0 copy-start
  0.0 0.7 copy-done
  0.7 10.0 %convolution_convert_fusion = bf16[16,12,3,128,64]{3,4,2,1,0:T(8,128)(2,1)} fusion(bf16[16,12,3,64,128]{4,3,2,1,0:T(8,128)(2,1)} %bitcast.67, bf16[64,64]{1,0:T(8,128)(2,1)S(1)} %copy-done), kind=kOutput, calls=%fused_computation.44 | convolution fusion | flops 608698368 | bytes 18882560 | tf_op jit(solution)/shard_map/ml,rbflp->rbfmp/dot_general | solution.py:43
  10.8 6.4 all-to-all-start
  17.2 0.0 copy-done.4
  17.2 0.7 convert_rsqrt_fusion
  17.9 206.1 %all-to-all-done = bf16[16,12,192,128]{3,2,1,0:T(8,128)(2,1)} async-done(((bf16[16,12,192,128]{3,2,1,0:T(8,128)(2,1)}), bf16[16,12,192,128]{3,2,1,0:T(8,128)(2,1)}, u32[]{:S(2)}, u32[]{:S(2)}) %all-to-all-start) | async-done | bytes 9437216 | tf_op jit(solution)/shard_map/all_to_all | solution.py:46
  224.0 10.0 %copy.11 = bf16[4,4,12,192,128]{4,3,2,0,1:T(8,128)(2,1)} copy(bf16[4,4,12,192,128]{4,3,2,1,0:T(8,128)(2,1)} %bitcast.6) | data formatting | bytes 18874368 | tf_op jit(solution)/shard_map/all_to_all | solution.py:46
  234.0 0.0 copy-done.2
  234.0 306.2 %while.15 = (s32[]{:T(128)}, f32[192,4,2,1280]{3,0,2,1:T(8,128)}, s32[4]{0:T(128)S(1)}, s32[1280]{0:T(1024)S(1)}, f32[4,1,1]{0,2,1:T(1,128)S(1)}, /*index=5*/bf1...) while((s32[]{:T(128)}, f32[192,4,2,1280]{3,0,2,1:T(8,128)}, ...), condition=%wide.region_1.2_spmd.clone, body=%wide.region_0.1_spmd.clone.sunk | while | flops 6199793152 | bytes 93940160 | solution.py:61
  250.8 0.1 broadcast_multiply_fusion.2
  251.0 4.3 fusion.39
  255.4 34.0 %fusion.38 = (f32[4,128,1280]{2,1,0:T(8,128)S(1)}, f32[4,128,1280]{2,1,0:T(8,128)S(1)}) fusion(f32[4]{0:T(128)S(1)} %divide_bitcast_fusion.2, s32[4]{0:T(128)S(1)} %compare_select_fusion.2, s32[128,1280]{1,0:T(8,128)S(1)} %iota_multiply_fusion.2, pred[4]{0:T(512)(128)(4,1)S(1)} %broadcast_compare_fusion.4), kind=kLoop, calls=%fused_computation.14.clone.1 | loop fusion | flops 5898240 | bytes 5898276 | tf_op jit(solution)/shard_map/while/body/eval_jaxpr/vmap()/cos | solution.py:18
  289.4 0.1 broadcast_compare_fusion.5
  289.4 14.5 %select_convert_fusion.4 = (bf16[4,12,128,1,1280]{4,2,1,3,0:T(8,128)(2,1)}, bf16[4,12,128,1,1280]{4,2,1,3,0:T(8,128)(2,1)}) fusion(f32[4,128,1280]{2,1,0:T(8,128)S(1)} %get-tuple-element.209, f32[4,12,1280]{2,1,0:T(8,128)S(1)} %get-tuple-element.210, f32[4,128,1280]{2,1,0:T(8,128)S(1)} %get-tuple-element.211, ...), kind=kLoop, calls=%fused_computation.5.clone.1 | loop fusion | flops 86507520 | bytes 37197824 | tf_op jit(solution)/shard_map/convert
  303.9 16.0 %bitcast_add_fusion.2 = f32[192,4,2,1280]{3,0,2,1:T(8,128)} fusion(f32[192,4,2,1280]{3,0,2,1:T(8,128)} %get-tuple-element.227, bf16[4,12,128,1,1280]{4,2,1,3,0:T(8,128)(2,1)} %get-tuple-element.213, bf16[4,12,128,1,1280]{4,2,1,3,0:T(8,128)(2,1)} %get-tuple-element.214, pred[]{:T(512)S(6)} %compare.3, ...), kind=kOutput, calls=%fused_computation.6.clone.1 | convolution fusion | flops 6106644480 | bytes 49545220 | tf_op jit(solution)/shard_map/while/body/eval_jaxpr/rbcp,rbpqs->crqs/dot_general | solution.py:55
  319.9 0.1 broadcast_multiply_fusion.2
  320.0 4.3 fusion.39
  324.4 34.0 %fusion.38 = (f32[4,128,1280]{2,1,0:T(8,128)S(1)}, f32[4,128,1280]{2,1,0:T(8,128)S(1)}) fusion(f32[4]{0:T(128)S(1)} %divide_bitcast_fusion.2, s32[4]{0:T(128)S(1)} %compare_select_fusion.2, s32[128,1280]{1,0:T(8,128)S(1)} %iota_multiply_fusion.2, pred[4]{0:T(512)(128)(4,1)S(1)} %broadcast_compare_fusion.4), kind=kLoop, calls=%fused_computation.14.clone.1 | loop fusion | flops 5898240 | bytes 5898276 | tf_op jit(solution)/shard_map/while/body/eval_jaxpr/vmap()/cos | solution.py:18
  358.4 0.1 broadcast_compare_fusion.5
  358.5 14.5 %select_convert_fusion.4 = (bf16[4,12,128,1,1280]{4,2,1,3,0:T(8,128)(2,1)}, bf16[4,12,128,1,1280]{4,2,1,3,0:T(8,128)(2,1)}) fusion(f32[4,128,1280]{2,1,0:T(8,128)S(1)} %get-tuple-element.209, f32[4,12,1280]{2,1,0:T(8,128)S(1)} %get-tuple-element.210, f32[4,128,1280]{2,1,0:T(8,128)S(1)} %get-tuple-element.211, ...), kind=kLoop, calls=%fused_computation.5.clone.1 | loop fusion | flops 86507520 | bytes 37197824 | tf_op jit(solution)/shard_map/convert
  373.0 17.6 %bitcast_add_fusion.2 = f32[192,4,2,1280]{3,0,2,1:T(8,128)} fusion(f32[192,4,2,1280]{3,0,2,1:T(8,128)} %get-tuple-element.227, bf16[4,12,128,1,1280]{4,2,1,3,0:T(8,128)(2,1)} %get-tuple-element.213, bf16[4,12,128,1,1280]{4,2,1,3,0:T(8,128)(2,1)} %get-tuple-element.214, pred[]{:T(512)S(6)} %compare.3, ...), kind=kOutput, calls=%fused_computation.6.clone.1 | convolution fusion | flops 6106644480 | bytes 49545220 | tf_op jit(solution)/shard_map/while/body/eval_jaxpr/rbcp,rbpqs->crqs/dot_general | solution.py:55
  390.5 0.1 broadcast_multiply_fusion.2
  390.6 4.3 fusion.39
  395.0 34.0 %fusion.38 = (f32[4,128,1280]{2,1,0:T(8,128)S(1)}, f32[4,128,1280]{2,1,0:T(8,128)S(1)}) fusion(f32[4]{0:T(128)S(1)} %divide_bitcast_fusion.2, s32[4]{0:T(128)S(1)} %compare_select_fusion.2, s32[128,1280]{1,0:T(8,128)S(1)} %iota_multiply_fusion.2, pred[4]{0:T(512)(128)(4,1)S(1)} %broadcast_compare_fusion.4), kind=kLoop, calls=%fused_computation.14.clone.1 | loop fusion | flops 5898240 | bytes 5898276 | tf_op jit(solution)/shard_map/while/body/eval_jaxpr/vmap()/cos | solution.py:18
  429.0 0.1 broadcast_compare_fusion.5
  429.1 14.5 %select_convert_fusion.4 = (bf16[4,12,128,1,1280]{4,2,1,3,0:T(8,128)(2,1)}, bf16[4,12,128,1,1280]{4,2,1,3,0:T(8,128)(2,1)}) fusion(f32[4,128,1280]{2,1,0:T(8,128)S(1)} %get-tuple-element.209, f32[4,12,1280]{2,1,0:T(8,128)S(1)} %get-tuple-element.210, f32[4,128,1280]{2,1,0:T(8,128)S(1)} %get-tuple-element.211, ...), kind=kLoop, calls=%fused_computation.5.clone.1 | loop fusion | flops 86507520 | bytes 37197824 | tf_op jit(solution)/shard_map/convert
  443.6 17.6 %bitcast_add_fusion.2 = f32[192,4,2,1280]{3,0,2,1:T(8,128)} fusion(f32[192,4,2,1280]{3,0,2,1:T(8,128)} %get-tuple-element.227, bf16[4,12,128,1,1280]{4,2,1,3,0:T(8,128)(2,1)} %get-tuple-element.213, bf16[4,12,128,1,1280]{4,2,1,3,0:T(8,128)(2,1)} %get-tuple-element.214, pred[]{:T(512)S(6)} %compare.3, ...), kind=kOutput, calls=%fused_computation.6.clone.1 | convolution fusion | flops 6106644480 | bytes 49545220 | tf_op jit(solution)/shard_map/while/body/eval_jaxpr/rbcp,rbpqs->crqs/dot_general | solution.py:55
  461.2 0.1 broadcast_multiply_fusion.2
  461.3 4.3 fusion.39
  465.7 34.0 %fusion.38 = (f32[4,128,1280]{2,1,0:T(8,128)S(1)}, f32[4,128,1280]{2,1,0:T(8,128)S(1)}) fusion(f32[4]{0:T(128)S(1)} %divide_bitcast_fusion.2, s32[4]{0:T(128)S(1)} %compare_select_fusion.2, s32[128,1280]{1,0:T(8,128)S(1)} %iota_multiply_fusion.2, pred[4]{0:T(512)(128)(4,1)S(1)} %broadcast_compare_fusion.4), kind=kLoop, calls=%fused_computation.14.clone.1 | loop fusion | flops 5898240 | bytes 5898276 | tf_op jit(solution)/shard_map/while/body/eval_jaxpr/vmap()/cos | solution.py:18
  499.7 0.1 broadcast_compare_fusion.5
  499.7 14.5 %select_convert_fusion.4 = (bf16[4,12,128,1,1280]{4,2,1,3,0:T(8,128)(2,1)}, bf16[4,12,128,1,1280]{4,2,1,3,0:T(8,128)(2,1)}) fusion(f32[4,128,1280]{2,1,0:T(8,128)S(1)} %get-tuple-element.209, f32[4,12,1280]{2,1,0:T(8,128)S(1)} %get-tuple-element.210, f32[4,128,1280]{2,1,0:T(8,128)S(1)} %get-tuple-element.211, ...), kind=kLoop, calls=%fused_computation.5.clone.1 | loop fusion | flops 86507520 | bytes 37197824 | tf_op jit(solution)/shard_map/convert
  514.2 17.6 %bitcast_add_fusion.2 = f32[192,4,2,1280]{3,0,2,1:T(8,128)} fusion(f32[192,4,2,1280]{3,0,2,1:T(8,128)} %get-tuple-element.227, bf16[4,12,128,1,1280]{4,2,1,3,0:T(8,128)(2,1)} %get-tuple-element.213, bf16[4,12,128,1,1280]{4,2,1,3,0:T(8,128)(2,1)} %get-tuple-element.214, pred[]{:T(512)S(6)} %compare.3, ...), kind=kOutput, calls=%fused_computation.6.clone.1 | convolution fusion | flops 6106644480 | bytes 49545220 | tf_op jit(solution)/shard_map/while/body/eval_jaxpr/rbcp,rbpqs->crqs/dot_general | solution.py:55
  540.2 0.0 copy-done.3
  540.2 5.8 multiply_convert_fusion
  546.0 11.6 %reshape.287 = bf16[4,48,4,2,8,160]{5,4,1,0,3,2:T(8,128)(2,1)} reshape(bf16[192,4,2,1280]{3,0,2,1:T(8,128)(2,1)} %multiply_convert_fusion) | data formatting | bytes 7864320 | tf_op jit(solution)/shard_map/reshape | solution.py:65
  557.6 13.6 %copy.25 = bf16[4,48,4,2,8,160]{5,0,4,1,3,2:T(4,128)(2,1)} copy(bf16[4,48,4,2,8,160]{5,4,1,0,3,2:T(8,128)(2,1)} %reshape.287) | data formatting | bytes 7864320 | tf_op jit(solution)/shard_map/reshape | solution.py:65
  571.2 41.1 %copy.21 = bf16[48,4,2,8,4,160]{0,2,1,5,4,3:T(2,128)(2,1)} copy(bf16[48,4,2,8,4,160]{5,4,3,0,2,1:T(4,128)(2,1)} %bitcast.65) | data formatting | bytes 7864320 | tf_op jit(solution)/shard_map/reshape | solution.py:67
  612.3 19.0 %reshape.293 = bf16[32,2,30720]{2,1,0:T(2,128)(2,1)} reshape(bf16[5120,4,2,48]{3,2,1,0:T(2,128)(2,1)} %bitcast.62) | data formatting | bytes 7864320
  631.3 3.8 all-to-all-start.1
  635.1 0.1 dynamic_slice.14
  635.2 0.2 iota_compare_fusion
  635.4 86.5 %all-to-all-done.1 = bf16[32,2,30720]{2,1,0:T(2,128)(2,1)} async-done(((bf16[32,2,30720]{2,1,0:T(2,128)(2,1)}), bf16[32,2,30720]{2,1,0:T(2,128)(2,1)}, u32[]{:S(2)}, u32[]{:S(2)}) %all-to-all-start.1) | async-done | bytes 3932192 | tf_op jit(solution)/shard_map/all_to_all | solution.py:68
  721.9 15.7 %reshape.294 = bf16[5120,4,2,48]{3,2,1,0:T(2,128)(2,1)} reshape(bf16[32,2,30720]{2,1,0:T(2,128)(2,1)} %all-to-all-done.1) | data formatting | bytes 7864320
  737.6 21.9 %copy.23 = bf16[48,4,2,32,160]{4,0,2,1,3:T(8,128)(2,1)} copy(bf16[48,4,2,32,160]{0,2,1,4,3:T(2,128)(2,1)} %bitcast.63) | data formatting | bytes 7864320 | tf_op jit(solution)/shard_map/all_to_all | solution.py:68
  759.5 9.3 %copy.16 = bf16[48,128,2,160]{1,0,2,3:T(8,128)(2,1)} copy(bf16[48,128,2,160]{3,0,2,1:T(8,128)(2,1)} %bitcast.66) | data formatting | bytes 7864320 | tf_op jit(solution)/shard_map/all_to_all | solution.py:68
  768.8 33.8 %fusion.26 = bf16[160,2,48,1280]{3,2,1,0:T(8,128)(2,1)} fusion(bf16[48,128,2,160]{1,0,2,3:T(8,128)(2,1)} %copy.16, bf16[160,128,1280]{2,1,0:T(8,128)(2,1)} %param.11, pred[160,1280]{1,0:T(8,128)(4,1)S(1)} %iota_compare_fusion), kind=kOutput, calls=%fused_computation.42 | convolution fusion | flops 5072486400 | bytes 95887360 | tf_op jit(solution)/shard_map/crqs,srn->sqcn/dot_general | solution.py:72
  (31 shorter events, 0.3 us)
Async XLA Ops:
  0.0 0.7 copy-start
  10.8 6.4 copy-start.4
  10.8 213.2 %all-to-all-start = ((bf16[16,12,192,128]{3,2,1,0:T(8,128)(2,1)}), bf16[16,12,192,128]{3,2,1,0:T(8,128)(2,1)}, u32[]{:S(2)}, u32[]{:S(2)}) async-start(bf16[16,12,192,128]{3,2,1,0:T(8,128)(2,1)} %bitcast.64), calls=%async_computation | async-start | bytes 18874368 | tf_op jit(solution)/shard_map/all_to_all | solution.py:46
  224.0 10.0 %copy-start.2 = (s32[1280]{0:T(1024)S(1)}, s32[1280]{0:T(1024)}, u32[]{:S(2)}) copy-start(s32[1280]{0:T(1024)} %param.10) | copy-start | bytes 15364
  234.0 306.2 %copy-start.3 = (f32[4]{0:T(128)S(1)}, f32[4]{0:T(128)}, u32[]{:S(2)}) copy-start(f32[4]{0:T(128)} %get-tuple-element.158) | copy-start | bytes 52
  631.3 90.6 %all-to-all-start.1 = ((bf16[32,2,30720]{2,1,0:T(2,128)(2,1)}), bf16[32,2,30720]{2,1,0:T(2,128)(2,1)}, u32[]{:S(2)}, u32[]{:S(2)}) async-start(bf16[32,2,30720]{2,1,0:T(2,128)(2,1)} %reshape.293), calls=%async_computation.1 | async-start | bytes 7864320 | tf_op jit(solution)/shard_map/all_to_all | solution.py:68
  768.8 33.9 %copy-start.1 = (bf16[64,64]{1,0:T(8,128)(2,1)S(1)}, bf16[64,64]{1,0:T(8,128)(2,1)}, u32[]{:S(2)}) copy-start(bf16[64,64]{1,0:T(8,128)(2,1)} %param.8) | copy-start | bytes 24580
where the time goes:
time: 812 us; the launch traced here: 803 us
  waiting for transfers between devices  293 us (36%)
  other arithmetic  219 us (27%)
  local copies, waits for them, and re-layouts  143 us (18%)
  matrix products  113 us (14%)
  loops' own time  25.4 us (3%)
  starting transfers between devices  10.3 us (1%)
    all_to_all x1, waiting for transfers between devices, per_device(): lax.all_to_all(lifted, 'lev', split_axis=0, concat_axis=1, tiled=True)  206 us
    cos x4, other arithmetic, fourier_table(): inner_cos = jnp.cos(inner_angle)[None, :, :]  136 us
    all_to_all x1, waiting for transfers between devices, per_device(): lax.all_to_all(arranged, ('band', 'lev'), split_axis=3, concat_axis=1, ti...  86.5 us
    dot_general x4, matrix products, add_group(): jnp.einsum('rbcp,rbpqs->crqs', group_piece, fourier, preferred_element_ty...  68.7 us
    another operation x4, other arithmetic  57.9 us
    reshape x1, local copies, waits for them, and re-layouts, per_device(): arranged.reshape(chan_share, my_rows, 2, band_count * lev_count * slots_h...  41.1 us
    unnamed x12, local copies, waits for them, and re-layouts  35.4 us
    dot_general x1, matrix products, per_device(): jnp.einsum('crqs,srn->sqcn', owned, legendre, preferred_element_type=jnp....  33.8 us
  transfers between devices with their start and end apart: 2, of which 2 were waited for; matrix products, arithmetic and copies ran while one was open for 0% of the time, Pallas kernels for 0%

commit v1 on v0

v1 whole, which is shorter than its diff:
```python
import functools
import math

import jax
import jax.numpy as jnp
from jax import lax
from jax.experimental import pallas as pl
from jax.experimental.pallas import tpu as pltpu
from jax.sharding import PartitionSpec as P

CHUNKS = 2
LONGEST = 5136
FINE = 16
COARSE = 32
SPAN = FINE * COARSE
TILE = 256
SLOTS = 4


def lift_kernel(scal_ref, w_ref, x_ref, o_ref, *, row_at, rows):
    length = scal_ref[row_at + pl.program_id(0)]
    first = scal_ref[rows]
    targets, _, blocks, share, width = o_ref.shape
    for b in range(0, blocks, 2):
        pair = jnp.concatenate([x_ref[0, b], x_ref[0, b + 1]], axis=1)
        y = jnp.dot(w_ref[...], pair, preferred_element_type=jnp.float32)
        spot = first + b * width + lax.broadcasted_iota(jnp.int32, y.shape, 1)
        y = jnp.where(spot < length, y, 0.0)
        for h in range(2):
            part = y[:, h * width : (h + 1) * width].reshape(targets, share, width)
            o_ref[:, 0, b + h] = part.astype(jnp.bfloat16)


def lift(columns, weight, scal, row_at, rows_part, targets):
    rows, blocks, channels, width = columns.shape
    share = channels // targets
    return pl.pallas_call(
        functools.partial(lift_kernel, row_at=row_at, rows=rows),
        grid_spec=pltpu.PrefetchScalarGridSpec(
            num_scalar_prefetch=1,
            grid=(rows_part,),
            in_specs=[
                pl.BlockSpec((channels, channels), lambda i, s: (0, 0)),
                pl.BlockSpec((1, blocks, channels, width), lambda i, s: (row_at + i, 0, 0, 0)),
            ],
            out_specs=pl.BlockSpec((targets, 1, blocks, share, width), lambda i, s: (0, i, 0, 0, 0)),
        ),
        out_shape=jax.ShapeDtypeStruct((targets, rows_part, blocks, share, width), jnp.bfloat16),
        compiler_params=pltpu.CompilerParams(vmem_limit_bytes=48 * 2**20),
        cost_estimate=pl.CostEstimate(
            flops=2 * rows_part * blocks * channels * channels * width,
            bytes_accessed=4 * rows_part * blocks * channels * width,
            transcendentals=0,
        ),
        name="lift",
    )(scal, weight, columns)


def turn(angle_half):
    h = angle_half
    g = h * h
    s = 1.0
    for k in (6, 5, 4, 3, 2, 1):
        s = 1.0 - s * g * (1.0 / ((2 * k) * (2 * k + 1)))
    c = 1.0
    for k in (7, 6, 5, 4, 3, 2, 1):
        c = 1.0 - c * g * (1.0 / ((2 * k - 1) * (2 * k)))
    s = s * h
    return 1.0 - 2.0 * s * s, 2.0 * s * c


def fourier_kernel(scal_ref, wave_ref, x_ref, o_ref, keep_ref, *, row_at, groups):
    row = pl.program_id(1)
    rows_part = pl.num_programs(1)
    sources, _, blocks, share, width = x_ref.shape
    per = SPAN // width
    length = jnp.full((1, TILE), scal_ref[row_at + row], jnp.int32).astype(jnp.float32)
    inverse = 1.0 / length
    waves = wave_ref[...].astype(jnp.float32)

    at = lax.broadcasted_iota(jnp.int32, (FINE + COARSE + 16, TILE), 0)
    step = jnp.where(
        at < FINE, at, jnp.where(at < FINE + COARSE, (at - FINE) * FINE, (at - FINE - COARSE) * SPAN)
    ).astype(jnp.float32)
    product = step * waves
    residue = product - jnp.floor(product * inverse + 0.5) * length
    cosine, sine = turn(residue * inverse * math.pi)

    fine_cos, fine_sin = cosine[:FINE][None], sine[:FINE][None]
    coarse_cos = cosine[FINE : FINE + COARSE][:, None, :]
    coarse_sin = sine[FINE : FINE + COARSE][:, None, :]
    table_cos = (coarse_cos * fine_cos - coarse_sin * fine_sin).reshape(SPAN, TILE)
    table_sin = (coarse_sin * fine_cos + coarse_cos * fine_sin).reshape(SPAN, TILE)
    table = jnp.concatenate([table_cos.astype(jnp.bfloat16), table_sin.astype(jnp.bfloat16)], axis=1)

    x = x_ref[...].reshape(sources * blocks, share, width)[: groups * per]
    x = x.reshape(groups, per, share, width)
    if share % 16:
        x = x.astype(jnp.float32)
    x = jnp.concatenate([x[:, j].reshape(groups * share, width) for j in range(per)], axis=1)
    y = jnp.dot(x.astype(jnp.bfloat16), table, preferred_element_type=jnp.float32)
    y = y.reshape(groups, share, 2 * TILE)

    real = jnp.zeros((share, TILE), jnp.float32)
    imag = jnp.zeros((share, TILE), jnp.float32)
    for g in range(groups):
        k = FINE + COARSE + g
        c, s = cosine[k : k + 1], sine[k : k + 1]
        a, b = y[g, :, :TILE], y[g, :, TILE:]
        real = real + (c * a - s * b)
        imag = imag - (s * a + c * b)
    scale = lax.rsqrt(length)
    lanes = keep_ref.shape[1]
    fill = jnp.zeros((lanes - 2 * share, TILE), jnp.float32)
    both = jnp.concatenate([real * scale, imag * scale, fill], axis=0)
    rows_static = o_ref.shape[1]
    keep_ref[pl.ds(row, TILE, stride=rows_static), :] = both.T

    @pl.when(row == rows_part - 1)
    def _():
        o_ref[...] = keep_ref[...].reshape(o_ref.shape).astype(jnp.bfloat16)


def fourier(points, wave_order, scal, row_at):
    sources, rows_part, blocks, share, width = points.shape
    wave_count = wave_order.shape[0]
    total = sources * blocks * width
    groups = min(-(-LONGEST // SPAN), total // SPAN)
    lanes = -(-2 * share // 128) * 128
    return pl.pallas_call(
        functools.partial(fourier_kernel, row_at=row_at, groups=groups),
        grid_spec=pltpu.PrefetchScalarGridSpec(
            num_scalar_prefetch=1,
            grid=(wave_count // TILE, rows_part),
            in_specs=[
                pl.BlockSpec((1, TILE), lambda t, i, s: (0, t)),
                pl.BlockSpec((sources, 1, blocks, share, width), lambda t, i, s: (0, i, 0, 0, 0)),
            ],
            out_specs=pl.BlockSpec((TILE, rows_part, lanes), lambda t, i, s: (t, 0, 0)),
            scratch_shapes=[pltpu.VMEM((TILE * rows_part, lanes), jnp.float32)],
        ),
        out_shape=jax.ShapeDtypeStruct((wave_count, rows_part, lanes), jnp.bfloat16),
        compiler_params=pltpu.CompilerParams(vmem_limit_bytes=48 * 2**20),
        cost_estimate=pl.CostEstimate(
            flops=4 * rows_part * groups * SPAN * share * wave_count,
            bytes_accessed=2 * rows_part * wave_count * (lanes + total * share // TILE),
            transcendentals=0,
        ),
        name="fourier",
    )(scal, wave_order.reshape(1, wave_count), points)


def legendre_kernel(wave_ref, table_ref, *refs):
    pieces, o_ref = refs[:-1], refs[-1]
    slots, _, share, degrees = o_ref.shape
    _, rows, _ = table_ref.shape
    lanes = pieces[0].shape[-1]
    degree = lax.broadcasted_iota(jnp.int32, (2 * share, degrees), 1)
    for k in range(slots):
        parts = [p[:, k][:, None].astype(jnp.float32) for p in pieces]
        x = jnp.concatenate(parts, axis=1).reshape(rows, lanes)
        x = x.T[: 2 * share].astype(jnp.bfloat16)
        y = jnp.dot(x, table_ref[k], preferred_element_type=jnp.float32)
        y = jnp.where(degree >= wave_ref[pl.program_id(0) * slots + k], y, 0.0)
        o_ref[k, 0] = y[:share].astype(jnp.bfloat16)
        o_ref[k, 1] = y[share:].astype(jnp.bfloat16)


def legendre_sum(own_waves, legendre, pieces, share):
    slots_here, rows, degrees = legendre.shape
    sources, _, rows_part, lanes = pieces[0].shape
    piece_spec = pl.BlockSpec((sources, SLOTS, rows_part, lanes), lambda i, w: (0, i, 0, 0))
    return pl.pallas_call(
        legendre_kernel,
        grid_spec=pltpu.PrefetchScalarGridSpec(
            num_scalar_prefetch=1,
            grid=(slots_here // SLOTS,),
            in_specs=[pl.BlockSpec((SLOTS, rows, degrees), lambda i, w: (i, 0, 0))]
            + [piece_spec] * len(pieces),
            out_specs=pl.BlockSpec((SLOTS, 2, share, degrees), lambda i, w: (i, 0, 0, 0)),
        ),
        out_shape=jax.ShapeDtypeStruct((slots_here, 2, share, degrees), jnp.bfloat16),
        compiler_params=pltpu.CompilerParams(vmem_limit_bytes=48 * 2**20),
        cost_estimate=pl.CostEstimate(
            flops=4 * slots_here * rows * share * degrees,
            bytes_accessed=2 * slots_here * degrees * (rows + 2 * share),
            transcendentals=0,
        ),
        name="legendre",
    )(own_waves, legendre, *pieces)


def per_device(columns, vertical, row_len, wave_order, legendre):
    rows_here, blocks_here, channels, width = columns.shape
    levels = vertical.shape[0]
    wave_count = wave_order.shape[0]
    bands = lax.axis_size("band")
    levs = lax.axis_size("lev")
    slots_here = legendre.shape[0]
    share = channels // levs
    first = lax.axis_index("lev") * (blocks_here * width)
    scal = jnp.concatenate([row_len, first.reshape(1).astype(jnp.int32)])
    weight = jnp.kron(jnp.eye(channels // levels, dtype=vertical.dtype), vertical)
    own_waves = lax.dynamic_slice_in_dim(wave_order, lax.axis_index("band") * slots_here, slots_here)
    rows_part = rows_here // CHUNKS
    pieces = []
    for part in range(CHUNKS):
        lifted = lift(columns, weight, scal, part * rows_part, rows_part, levs)
        points = lax.all_to_all(lifted, "lev", split_axis=0, concat_axis=0, tiled=True)
        coeffs = fourier(points, wave_order, scal, part * rows_part)
        coeffs = coeffs.reshape(bands, slots_here, rows_part, coeffs.shape[-1])
        pieces.append(lax.all_to_all(coeffs, "band", split_axis=0, concat_axis=0, tiled=True))
    return legendre_sum(own_waves, legendre, pieces, share)


def solution(mesh):
    return jax.shard_map(
        per_device,
        mesh=mesh,
        in_specs=(P("band", "lev", None, None), P(), P("band"), P(), P("band", None, None)),
        out_specs=P("band", None, "lev", None),
        check_vma=False,
    )
```

time: 812 us -> 365 us (0.45)
  other arithmetic: 219 us -> 1.59 us
  Pallas kernels: 0 us -> 141 us
  local copies, waits for them, and re-layouts: 143 us -> 7.57 us
  matrix products: 113 us -> 0 us
  waiting for transfers between devices: 293 us -> 192 us
  loops' own time: 25.4 us -> 0 us
  starting transfers between devices: 10.3 us -> 19.5 us
    cos x8 -> x0, other arithmetic: 153 us -> none  [the longest x4 136 us: fourier_table(): inner_cos = jnp.cos(inner_angle)[None, :, :]]
    pallas_call x0 -> x5, Pallas kernels: none -> 141 us  [the longest x2 75.9 us: fourier(): pl.pallas_call(functools.partial(fourier_kernel, row_at=row_at, groups=gr...]
    dot_general x6 -> x0, matrix products: 113 us -> none  [the longest x4 68.7 us: add_group(): jnp.einsum('rbcp,rbpqs->crqs', group_piece, fourier, preferred_element_ty...]
    all_to_all x2 -> x4, waiting for transfers between devices: 293 us -> 192 us  [the longest x2 160 us: per_device(): lax.all_to_all(lifted, 'lev', split_axis=0, concat_axis=0, tiled=True)]
    reshape x3 -> x1, local copies, waits for them, and re-layouts: 66.3 us -> 0.01 us  [fourier(): wave_order.reshape(1, wave_count)]
    another operation x4 -> x0, other arithmetic: 57.9 us -> none
    all_to_all x3 -> x0, local copies, waits for them, and re-layouts: 41.2 us -> none  [the longest x2 31.2 us: per_device(): lax.all_to_all(arranged, ('band', 'lev'), split_axis=3, concat_axis=1, ti...]
    unnamed x12 -> x10, local copies, waits for them, and re-layouts: 35.4 us -> 7.32 us
  transfers between devices with their start and end apart: 2 -> 4, of which waited for: 2 -> 3; matrix products, arithmetic and copies ran while one was open for 0% -> 0% of each run, Pallas kernels for 0% -> 23%
where the time goes in v1:
time: 365 us; the launch traced here: 362 us
  waiting for transfers between devices  192 us (53%)
  Pallas kernels  141 us (39%)
  starting transfers between devices  19.5 us (5%)
  local copies, waits for them, and re-layouts  7.57 us (2%)
    all_to_all x2, waiting for transfers between devices, per_device(): lax.all_to_all(lifted, 'lev', split_axis=0, concat_axis=0, tiled=True)  160 us
    pallas_call x2, Pallas kernels, fourier(): pl.pallas_call(functools.partial(fourier_kernel, row_at=row_at, groups=gr...  75.9 us
    pallas_call x1, Pallas kernels, legendre_sum(): pl.pallas_call(legendre_kernel, grid_spec=pltpu.PrefetchScalarGridSpec(nu...  51.5 us
    all_to_all x2, waiting for transfers between devices, per_device(): lax.all_to_all(coeffs, 'band', split_axis=0, concat_axis=0, tiled=True)  32.2 us
    pallas_call x2, Pallas kernels, lift(): pl.pallas_call(functools.partial(lift_kernel, row_at=row_at, rows=rows),...  13.4 us
    all_to_all x2, starting transfers between devices, per_device(): lax.all_to_all(lifted, 'lev', split_axis=0, concat_axis=0, tiled=True)  11.3 us
    all_to_all x2, starting transfers between devices, per_device(): lax.all_to_all(coeffs, 'band', split_axis=0, concat_axis=0, tiled=True)  8.18 us
    unnamed x10, local copies, waits for them, and re-layouts  7.32 us
  transfers between devices with their start and end apart: 4, of which 3 were waited for; matrix products, arithmetic and copies ran while one was open for 0% of the time, Pallas kernels for 23%

profile of v1, /device:TPU:0, one launch (start us, length us, event | category | flops | bytes accessed | tf_op | source)
XLA Modules:
  0.0 361.9 jit_solution(4063593423450376043)
XLA Ops:
  0.0 0.9 broadcast_multiply_fusion
  0.9 0.2 mul.35.w_ref
  1.0 0.7 pad_add_fusion.scal_ref
  1.8 6.7 %lift.3 = bf16[4,8,12,48,128]{4,3,2,1,0:T(8,128)(2,1)S(1)} custom-call(s32[17]{0:T(128)S(1)} %pad_add_fusion.scal_ref, bf16[192,192]{1,0:T(8,128)(2,1)S(1)} %mul.35.w_ref, bf16[16,12,192,128]{3,2,1,0:T(8,128)(2,1)} %x_ref.3), custom_call_target="tpu_custom_call" | custom-call | flops 905969664 | bytes 9437184 | tf_op jit(solution)/shard_map/lift/pallas_call | solution.py:37
  8.5 0.0 copy-start.1
  8.5 2.1 copy-done.1
  10.6 6.3 %all-to-all-start.2 = ((bf16[4,8,12,48,128]{4,3,2,1,0:T(8,128)(2,1)}), bf16[4,8,12,48,128]{4,3,2,1,0:T(8,128)(2,1)}, u32[]{:S(2)}, u32[]{:S(2)}) async-start(bf16[4,8,12,48,128]{4,3,2,1,0:T(8,128)(2,1)} %copy-done.1), calls=%async_computation.2 | async-start | bytes 9437184 | tf_op jit(solution)/shard_map/all_to_all | solution.py:209
  16.9 6.7 %lift.2 = bf16[4,8,12,48,128]{4,3,2,1,0:T(8,128)(2,1)S(1)} custom-call(s32[17]{0:T(128)S(1)} %pad_add_fusion.scal_ref, bf16[192,192]{1,0:T(8,128)(2,1)S(1)} %mul.35.w_ref, bf16[16,12,192,128]{3,2,1,0:T(8,128)(2,1)} %x_ref.3), custom_call_target="tpu_custom_call" | custom-call | flops 905969664 | bytes 9437184 | tf_op jit(solution)/shard_map/lift/pallas_call | solution.py:37
  23.6 0.0 copy-start
  23.7 2.2 copy-done
  25.8 0.0 copy-start.4
  25.8 95.9 %all-to-all-done.2.x_ref = bf16[4,8,12,48,128]{4,3,2,1,0:T(8,128)(2,1)} async-done(((bf16[4,8,12,48,128]{4,3,2,1,0:T(8,128)(2,1)}), bf16[4,8,12,48,128]{4,3,2,1,0:T(8,128)(2,1)}, u32[]{:S(2)}, u32[]{:S(2)}) %all-to-all-start.2) | async-done | bytes 4718624 | tf_op jit(solution)/shard_map/all_to_all | solution.py:209
  121.7 5.0 %all-to-all-start = ((bf16[4,8,12,48,128]{4,3,2,1,0:T(8,128)(2,1)}), bf16[4,8,12,48,128]{4,3,2,1,0:T(8,128)(2,1)}, u32[]{:S(2)}, u32[]{:S(2)}) async-start(bf16[4,8,12,48,128]{4,3,2,1,0:T(8,128)(2,1)} %copy-done), calls=%async_computation | async-start | bytes 9437184 | tf_op jit(solution)/shard_map/all_to_all | solution.py:209
  126.7 0.0 copy-done.4
  126.7 37.9 %fourier.3 = bf16[1280,8,128]{2,1,0:T(8,128)(2,1)S(1)} custom-call(s32[17]{0:T(128)S(1)} %pad_add_fusion.scal_ref, s32[1,1280]{1,0:T(1,128)S(1)} %reshape.28.wave_ref, bf16[4,8,12,48,128]{4,3,2,1,0:T(8,128)(2,1)} %all-to-all-done.2.x_ref), custom_call_target="tpu_custom_call" | custom-call | flops 11072962560 | bytes 26214400 | tf_op jit(solution)/shard_map/fourier/pallas_call | solution.py:130
  164.7 0.0 copy-start.3
  164.7 1.5 copy-done.3
  166.2 64.4 %all-to-all-done.x_ref = bf16[4,8,12,48,128]{4,3,2,1,0:T(8,128)(2,1)} async-done(((bf16[4,8,12,48,128]{4,3,2,1,0:T(8,128)(2,1)}), bf16[4,8,12,48,128]{4,3,2,1,0:T(8,128)(2,1)}, u32[]{:S(2)}, u32[]{:S(2)}) %all-to-all-start) | async-done | bytes 4718624 | tf_op jit(solution)/shard_map/all_to_all | solution.py:209
  230.5 3.8 %all-to-all-start.3 = ((bf16[8,160,8,128]{3,2,1,0:T(8,128)(2,1)}), bf16[8,160,8,128]{3,2,1,0:T(8,128)(2,1)S(1)}, u32[]{:S(2)}, u32[]{:S(2)}) async-start(bf16[8,160,8,128]{3,2,1,0:T(8,128)(2,1)} %bitcast.4), calls=%async_computation.3 | async-start | bytes 5242880 | tf_op jit(solution)/shard_map/all_to_all | solution.py:212
  234.3 38.0 %fourier.2 = bf16[1280,8,128]{2,1,0:T(8,128)(2,1)S(1)} custom-call(s32[17]{0:T(128)S(1)} %pad_add_fusion.scal_ref, s32[1,1280]{1,0:T(1,128)S(1)} %reshape.28.wave_ref, bf16[4,8,12,48,128]{4,3,2,1,0:T(8,128)(2,1)} %all-to-all-done.x_ref), custom_call_target="tpu_custom_call" | custom-call | flops 11072962560 | bytes 26214400 | tf_op jit(solution)/shard_map/fourier/pallas_call | solution.py:130
  272.3 0.0 copy-start.2
  272.3 1.5 copy-done.2
  273.8 0.0 all-to-all-done.3.refs_1_
  273.8 4.4 %all-to-all-start.1 = ((bf16[8,160,8,128]{3,2,1,0:T(8,128)(2,1)}), bf16[8,160,8,128]{3,2,1,0:T(8,128)(2,1)}, u32[]{:S(2)}, u32[]{:S(2)}) async-start(bf16[8,160,8,128]{3,2,1,0:T(8,128)(2,1)} %bitcast.3), calls=%async_computation.1 | async-start | bytes 5242880 | tf_op jit(solution)/shard_map/all_to_all | solution.py:212
  278.2 0.1 dynamic_slice.3.wave_ref
  278.3 32.2 %all-to-all-done.1.refs_0_ = bf16[8,160,8,128]{3,2,1,0:T(8,128)(2,1)} async-done(((bf16[8,160,8,128]{3,2,1,0:T(8,128)(2,1)}), bf16[8,160,8,128]{3,2,1,0:T(8,128)(2,1)}, u32[]{:S(2)}, u32[]{:S(2)}) %all-to-all-start.1) | async-done | bytes 2621472 | tf_op jit(solution)/shard_map/all_to_all | solution.py:212
  310.5 51.5 %legendre.1 = bf16[160,2,48,1280]{3,2,1,0:T(8,128)(2,1)} custom-call(s32[160]{0:T(256)S(1)} %dynamic_slice.3.wave_ref, bf16[160,128,1280]{2,1,0:T(8,128)(2,1)} %table_ref.1, bf16[8,160,8,128]{3,2,1,0:T(8,128)(2,1)} %all-to-all-done.1.refs_0_, bf16[8,160,8,128]{3,2,1,0:T(8,128)(2,1)S(1)} %all-to-all-done.3.refs_1_), custom_call_target="tpu_custom_call" | custom-call | flops 5033164800 | bytes 91750400 | tf_op jit(solution)/shard_map/legendre/pallas_call | solution.py:173
  (2 shorter events, 0.0 us)
Async XLA Ops:
  8.5 2.1 copy-start.1
  10.6 111.1 %all-to-all-start.2 = ((bf16[4,8,12,48,128]{4,3,2,1,0:T(8,128)(2,1)}), bf16[4,8,12,48,128]{4,3,2,1,0:T(8,128)(2,1)}, u32[]{:S(2)}, u32[]{:S(2)}) async-start(bf16[4,8,12,48,128]{4,3,2,1,0:T(8,128)(2,1)} %copy-done.1), calls=%async_computation.2 | async-start | bytes 9437184 | tf_op jit(solution)/shard_map/all_to_all | solution.py:209
  23.6 2.2 copy-start
  25.8 100.8 %copy-start.4 = (s32[1280]{0:T(1024)S(1)}, s32[1280]{0:T(1024)}, u32[]{:S(2)}) copy-start(s32[1280]{0:T(1024)} %param.8) | copy-start | bytes 15364
  121.7 108.8 %all-to-all-start = ((bf16[4,8,12,48,128]{4,3,2,1,0:T(8,128)(2,1)}), bf16[4,8,12,48,128]{4,3,2,1,0:T(8,128)(2,1)}, u32[]{:S(2)}, u32[]{:S(2)}) async-start(bf16[4,8,12,48,128]{4,3,2,1,0:T(8,128)(2,1)} %copy-done), calls=%async_computation | async-start | bytes 9437184 | tf_op jit(solution)/shard_map/all_to_all | solution.py:209
  164.7 1.5 copy-start.3
  230.5 43.3 %all-to-all-start.3 = ((bf16[8,160,8,128]{3,2,1,0:T(8,128)(2,1)}), bf16[8,160,8,128]{3,2,1,0:T(8,128)(2,1)S(1)}, u32[]{:S(2)}, u32[]{:S(2)}) async-start(bf16[8,160,8,128]{3,2,1,0:T(8,128)(2,1)} %bitcast.4), calls=%async_computation.3 | async-start | bytes 5242880 | tf_op jit(solution)/shard_map/all_to_all | solution.py:212
  272.3 1.5 copy-start.2
  273.8 36.7 %all-to-all-start.1 = ((bf16[8,160,8,128]{3,2,1,0:T(8,128)(2,1)}), bf16[8,160,8,128]{3,2,1,0:T(8,128)(2,1)}, u32[]{:S(2)}, u32[]{:S(2)}) async-start(bf16[8,160,8,128]{3,2,1,0:T(8,128)(2,1)} %bitcast.3), calls=%async_computation.1 | async-start | bytes 5242880 | tf_op jit(solution)/shard_map/all_to_all | solution.py:212

commit v2 on v1

--- a/solution.py
+++ b/solution.py
@@ -8,13 +8,13 @@
 from jax.experimental.pallas import tpu as pltpu
 from jax.sharding import PartitionSpec as P
 
-CHUNKS = 2
+PARTS = (2, 1, 1)
 LONGEST = 5136
 FINE = 16
 COARSE = 32
 SPAN = FINE * COARSE
-TILE = 256
-SLOTS = 4
+TILE = 640
+SLOTS = 20
 
 
 def lift_kernel(scal_ref, w_ref, x_ref, o_ref, *, row_at, rows):
@@ -143,7 +143,7 @@
         compiler_params=pltpu.CompilerParams(vmem_limit_bytes=48 * 2**20),
         cost_estimate=pl.CostEstimate(
             flops=4 * rows_part * groups * SPAN * share * wave_count,
-            bytes_accessed=2 * rows_part * wave_count * (lanes + total * share // TILE),
+            bytes_accessed=2 * rows_part * (wave_count * lanes + total * share * (wave_count // TILE)),
             transcendentals=0,
         ),
         name="fourier",
@@ -157,7 +157,7 @@
     lanes = pieces[0].shape[-1]
     degree = lax.broadcasted_iota(jnp.int32, (2 * share, degrees), 1)
     for k in range(slots):
-        parts = [p[:, k][:, None].astype(jnp.float32) for p in pieces]
+        parts = [p[:, k].astype(jnp.float32) for p in pieces]
         x = jnp.concatenate(parts, axis=1).reshape(rows, lanes)
         x = x.T[: 2 * share].astype(jnp.bfloat16)
         y = jnp.dot(x, table_ref[k], preferred_element_type=jnp.float32)
@@ -168,15 +168,16 @@
 
 def legendre_sum(own_waves, legendre, pieces, share):
     slots_here, rows, degrees = legendre.shape
-    sources, _, rows_part, lanes = pieces[0].shape
-    piece_spec = pl.BlockSpec((sources, SLOTS, rows_part, lanes), lambda i, w: (0, i, 0, 0))
+    piece_specs = [
+        pl.BlockSpec((p.shape[0], SLOTS, *p.shape[2:]), lambda i, w: (0, i, 0, 0)) for p in pieces
+    ]
     return pl.pallas_call(
         legendre_kernel,
         grid_spec=pltpu.PrefetchScalarGridSpec(
             num_scalar_prefetch=1,
             grid=(slots_here // SLOTS,),
             in_specs=[pl.BlockSpec((SLOTS, rows, degrees), lambda i, w: (i, 0, 0))]
-            + [piece_spec] * len(pieces),
+            + piece_specs,
             out_specs=pl.BlockSpec((SLOTS, 2, share, degrees), lambda i, w: (i, 0, 0, 0)),
         ),
         out_shape=jax.ShapeDtypeStruct((slots_here, 2, share, degrees), jnp.bfloat16),
@@ -202,12 +203,14 @@
     scal = jnp.concatenate([row_len, first.reshape(1).astype(jnp.int32)])
     weight = jnp.kron(jnp.eye(channels // levels, dtype=vertical.dtype), vertical)
     own_waves = lax.dynamic_slice_in_dim(wave_order, lax.axis_index("band") * slots_here, slots_here)
-    rows_part = rows_here // CHUNKS
     pieces = []
-    for part in range(CHUNKS):
-        lifted = lift(columns, weight, scal, part * rows_part, rows_part, levs)
+    row_at = 0
+    for part in PARTS:
+        rows_part = rows_here * part // sum(PARTS)
+        lifted = lift(columns, weight, scal, row_at, rows_part, levs)
         points = lax.all_to_all(lifted, "lev", split_axis=0, concat_axis=0, tiled=True)
-        coeffs = fourier(points, wave_order, scal, part * rows_part)
+        coeffs = fourier(points, wave_order, scal, row_at)
+        row_at += rows_part
         coeffs = coeffs.reshape(bands, slots_here, rows_part, coeffs.shape[-1])
         pieces.append(lax.all_to_all(coeffs, "band", split_axis=0, concat_axis=0, tiled=True))
     return legendre_sum(own_waves, legendre, pieces, share)

time: 365 us -> 363 us (level)
  Pallas kernels: 141 us -> 103 us
  waiting for transfers between devices: 192 us -> 214 us
  local copies, waits for them, and re-layouts: 7.57 us -> 16 us
  starting transfers between devices: 19.5 us -> 27.6 us
    pallas_call x2 -> x3, Pallas kernels: 75.9 us -> 53.9 us  [fourier(): pl.pallas_call(functools.partial(fourier_kernel, row_at=row_at, groups=gr...]
    pallas_call x1, Pallas kernels: 51.5 us -> 32.5 us  [legendre_sum(): pl.pallas_call(legendre_kernel, grid_spec=pltpu.PrefetchScalarGridSpec(nu...]
    all_to_all x2 -> x3, waiting for transfers between devices: 160 us -> 172 us  [per_device(): lax.all_to_all(lifted, 'lev', split_axis=0, concat_axis=0, tiled=True)]
    all_to_all x2 -> x3, waiting for transfers between devices: 32.2 us -> 41.5 us  [per_device(): lax.all_to_all(coeffs, 'band', split_axis=0, concat_axis=0, tiled=True)]
    unnamed x10 -> x24, local copies, waits for them, and re-layouts: 7.32 us -> 15.8 us
    all_to_all x2 -> x3, starting transfers between devices: 8.18 us -> 12.7 us  [per_device(): lax.all_to_all(coeffs, 'band', split_axis=0, concat_axis=0, tiled=True)]
    all_to_all x2 -> x3, starting transfers between devices: 11.3 us -> 14.9 us  [per_device(): lax.all_to_all(lifted, 'lev', split_axis=0, concat_axis=0, tiled=True)]
    pallas_call x2 -> x3, Pallas kernels: 13.4 us -> 16.6 us  [lift(): pl.pallas_call(functools.partial(lift_kernel, row_at=row_at, rows=rows),...]
  transfers between devices with their start and end apart: 4 -> 6, of which waited for: 3 -> 5; matrix products, arithmetic and copies ran while one was open for 0% -> 0% of each run, Pallas kernels for 23% -> 18%
where the time goes in v2:
time: 363 us; the launch traced here: 362 us
  waiting for transfers between devices  214 us (59%)
  Pallas kernels  103 us (28%)
  starting transfers between devices  27.6 us (8%)
  local copies, waits for them, and re-layouts  16 us (4%)
    all_to_all x3, waiting for transfers between devices, per_device(): lax.all_to_all(lifted, 'lev', split_axis=0, concat_axis=0, tiled=True)  172 us
    pallas_call x3, Pallas kernels, fourier(): pl.pallas_call(functools.partial(fourier_kernel, row_at=row_at, groups=gr...  53.9 us
    all_to_all x3, waiting for transfers between devices, per_device(): lax.all_to_all(coeffs, 'band', split_axis=0, concat_axis=0, tiled=True)  41.5 us
    pallas_call x1, Pallas kernels, legendre_sum(): pl.pallas_call(legendre_kernel, grid_spec=pltpu.PrefetchScalarGridSpec(nu...  32.5 us
    pallas_call x3, Pallas kernels, lift(): pl.pallas_call(functools.partial(lift_kernel, row_at=row_at, rows=rows),...  16.6 us
    unnamed x24, local copies, waits for them, and re-layouts  15.8 us
    all_to_all x3, starting transfers between devices, per_device(): lax.all_to_all(lifted, 'lev', split_axis=0, concat_axis=0, tiled=True)  14.9 us
    all_to_all x3, starting transfers between devices, per_device(): lax.all_to_all(coeffs, 'band', split_axis=0, concat_axis=0, tiled=True)  12.7 us
  transfers between devices with their start and end apart: 6, of which 5 were waited for; matrix products, arithmetic and copies ran while one was open for 0% of the time, Pallas kernels for 18%

profile of v2, /device:TPU:0, one launch (start us, length us, event | category | flops | bytes accessed | tf_op | source)
XLA Modules:
  0.0 362.0 jit_solution(12850185112013929179)
XLA Ops:
  0.0 0.9 broadcast_multiply_fusion
  0.9 0.2 mul.35.w_ref
  1.0 0.7 pad_add_fusion.scal_ref
  1.8 5.0 %lift.5 = bf16[4,4,12,48,128]{4,3,2,1,0:T(8,128)(2,1)} custom-call(s32[17]{0:T(128)S(1)} %pad_add_fusion.scal_ref, bf16[192,192]{1,0:T(8,128)(2,1)S(1)} %mul.35.w_ref, bf16[16,12,192,128]{3,2,1,0:T(8,128)(2,1)} %x_ref.5), custom_call_target="tpu_custom_call" | custom-call | flops 452984832 | bytes 4718592 | tf_op jit(solution)/shard_map/lift/pallas_call | solution.py:37
  6.7 6.3 %all-to-all-start.4 = ((bf16[4,4,12,48,128]{4,3,2,1,0:T(8,128)(2,1)}), bf16[4,4,12,48,128]{4,3,2,1,0:T(8,128)(2,1)S(1)}, u32[]{:S(2)}, u32[]{:S(2)}) async-start(bf16[4,4,12,48,128]{4,3,2,1,0:T(8,128)(2,1)} %lift.5), calls=%async_computation.4 | async-start | bytes 4718592 | tf_op jit(solution)/shard_map/all_to_all | solution.py:211
  13.1 5.0 %lift.4 = bf16[4,4,12,48,128]{4,3,2,1,0:T(8,128)(2,1)} custom-call(s32[17]{0:T(128)S(1)} %pad_add_fusion.scal_ref, bf16[192,192]{1,0:T(8,128)(2,1)S(1)} %mul.35.w_ref, bf16[16,12,192,128]{3,2,1,0:T(8,128)(2,1)} %x_ref.5), custom_call_target="tpu_custom_call" | custom-call | flops 452984832 | bytes 4718592 | tf_op jit(solution)/shard_map/lift/pallas_call | solution.py:37
  18.0 0.0 copy-start.11
  18.0 48.8 %all-to-all-done.4.x_ref = bf16[4,4,12,48,128]{4,3,2,1,0:T(8,128)(2,1)S(1)} async-done(((bf16[4,4,12,48,128]{4,3,2,1,0:T(8,128)(2,1)}), bf16[4,4,12,48,128]{4,3,2,1,0:T(8,128)(2,1)S(1)}, u32[]{:S(2)}, u32[]{:S(2)}) %all-to-all-start.4) | async-done | bytes 2359328 | tf_op jit(solution)/shard_map/all_to_all | solution.py:211
  66.9 0.0 copy-start.8
  66.9 1.4 copy-done.8
  68.3 3.6 %all-to-all-start.2 = ((bf16[4,4,12,48,128]{4,3,2,1,0:T(8,128)(2,1)}), bf16[4,4,12,48,128]{4,3,2,1,0:T(8,128)(2,1)S(1)}, u32[]{:S(2)}, u32[]{:S(2)}) async-start(bf16[4,4,12,48,128]{4,3,2,1,0:T(8,128)(2,1)} %lift.4), calls=%async_computation.2 | async-start | bytes 4718592 | tf_op jit(solution)/shard_map/all_to_all | solution.py:211
  72.0 0.0 copy-done.11
  72.0 0.0 copy-start.9
  72.0 1.7 copy-done.9
  73.6 13.3 %fourier.5 = bf16[1280,4,128]{2,1,0:T(4,128)(2,1)S(1)} custom-call(s32[17]{0:T(128)S(1)} %pad_add_fusion.scal_ref, s32[1,1280]{1,0:T(1,128)S(1)} %reshape.32.wave_ref, bf16[4,4,12,48,128]{4,3,2,1,0:T(8,128)(2,1)S(1)} %copy-done.9), custom_call_target="tpu_custom_call" | custom-call | flops 5536481280 | bytes 6029312 | tf_op jit(solution)/shard_map/fourier/pallas_call | solution.py:130
  87.0 0.0 copy-start.10
  87.0 1.1 copy-done.10
  88.0 37.2 %all-to-all-done.2.x_ref = bf16[4,4,12,48,128]{4,3,2,1,0:T(8,128)(2,1)S(1)} async-done(((bf16[4,4,12,48,128]{4,3,2,1,0:T(8,128)(2,1)}), bf16[4,4,12,48,128]{4,3,2,1,0:T(8,128)(2,1)S(1)}, u32[]{:S(2)}, u32[]{:S(2)}) %all-to-all-start.2) | async-done | bytes 2359328 | tf_op jit(solution)/shard_map/all_to_all | solution.py:211
  125.2 0.0 copy-start.6
  125.2 1.4 copy-done.6
  126.7 3.7 %all-to-all-start.5 = ((bf16[8,160,4,128]{3,2,1,0:T(4,128)(2,1)}), bf16[8,160,4,128]{3,2,1,0:T(4,128)(2,1)S(1)}, u32[]{:S(2)}, u32[]{:S(2)}) async-start(bf16[8,160,4,128]{3,2,1,0:T(4,128)(2,1)} %bitcast.5), calls=%async_computation.5 | async-start | bytes 2621440 | tf_op jit(solution)/shard_map/all_to_all | solution.py:215
  130.4 6.7 %lift.3 = bf16[4,8,12,48,128]{4,3,2,1,0:T(8,128)(2,1)S(1)} custom-call(s32[17]{0:T(128)S(1)} %pad_add_fusion.scal_ref, bf16[192,192]{1,0:T(8,128)(2,1)S(1)} %mul.35.w_ref, bf16[16,12,192,128]{3,2,1,0:T(8,128)(2,1)} %x_ref.5), custom_call_target="tpu_custom_call" | custom-call | flops 905969664 | bytes 9437184 | tf_op jit(solution)/shard_map/lift/pallas_call | solution.py:37
  137.1 0.0 copy-start
  137.1 2.2 copy-done
  139.3 9.3 %all-to-all-done.5.refs_2_ = bf16[8,160,4,128]{3,2,1,0:T(4,128)(2,1)S(1)} async-done(((bf16[8,160,4,128]{3,2,1,0:T(4,128)(2,1)}), bf16[8,160,4,128]{3,2,1,0:T(4,128)(2,1)S(1)}, u32[]{:S(2)}, u32[]{:S(2)}) %all-to-all-start.5) | async-done | bytes 1310752 | tf_op jit(solution)/shard_map/all_to_all | solution.py:215
  148.6 0.0 copy-start.1
  148.6 1.1 copy-done.1
  149.8 5.0 %all-to-all-start = ((bf16[4,8,12,48,128]{4,3,2,1,0:T(8,128)(2,1)}), bf16[4,8,12,48,128]{4,3,2,1,0:T(8,128)(2,1)}, u32[]{:S(2)}, u32[]{:S(2)}) async-start(bf16[4,8,12,48,128]{4,3,2,1,0:T(8,128)(2,1)} %copy-done), calls=%async_computation | async-start | bytes 9437184 | tf_op jit(solution)/shard_map/all_to_all | solution.py:211
  154.7 0.0 copy-start.7
  154.7 1.7 copy-done.7
  156.4 14.2 %fourier.4 = bf16[1280,4,128]{2,1,0:T(4,128)(2,1)} custom-call(s32[17]{0:T(128)S(1)} %pad_add_fusion.scal_ref, s32[1,1280]{1,0:T(1,128)S(1)} %reshape.32.wave_ref, bf16[4,4,12,48,128]{4,3,2,1,0:T(8,128)(2,1)S(1)} %copy-done.7), custom_call_target="tpu_custom_call" | custom-call | flops 5536481280 | bytes 6029312 | tf_op jit(solution)/shard_map/fourier/pallas_call | solution.py:130
  170.6 86.0 %all-to-all-done.x_ref = bf16[4,8,12,48,128]{4,3,2,1,0:T(8,128)(2,1)} async-done(((bf16[4,8,12,48,128]{4,3,2,1,0:T(8,128)(2,1)}), bf16[4,8,12,48,128]{4,3,2,1,0:T(8,128)(2,1)}, u32[]{:S(2)}, u32[]{:S(2)}) %all-to-all-start) | async-done | bytes 4718624 | tf_op jit(solution)/shard_map/all_to_all | solution.py:211
  256.7 4.8 %all-to-all-start.3 = ((bf16[8,160,4,128]{3,2,1,0:T(4,128)(2,1)}), bf16[8,160,4,128]{3,2,1,0:T(4,128)(2,1)S(1)}, u32[]{:S(2)}, u32[]{:S(2)}) async-start(bf16[8,160,4,128]{3,2,1,0:T(4,128)(2,1)} %bitcast.2), calls=%async_computation.3 | async-start | bytes 2621440 | tf_op jit(solution)/shard_map/all_to_all | solution.py:215
  261.5 26.4 %fourier.3 = bf16[1280,8,128]{2,1,0:T(8,128)(2,1)S(1)} custom-call(s32[17]{0:T(128)S(1)} %pad_add_fusion.scal_ref, s32[1,1280]{1,0:T(1,128)S(1)} %reshape.32.wave_ref, bf16[4,8,12,48,128]{4,3,2,1,0:T(8,128)(2,1)} %all-to-all-done.x_ref), custom_call_target="tpu_custom_call" | custom-call | flops 11072962560 | bytes 12058624 | tf_op jit(solution)/shard_map/fourier/pallas_call | solution.py:130
  287.9 0.0 copy-start.5
  287.9 1.5 copy-done.5
  289.4 0.0 all-to-all-done.3.refs_1_
  289.4 0.0 copy-start.3
  289.4 1.1 copy-done.3
  290.4 4.2 %all-to-all-start.1 = ((bf16[8,160,8,128]{3,2,1,0:T(8,128)(2,1)}), bf16[8,160,8,128]{3,2,1,0:T(8,128)(2,1)S(1)}, u32[]{:S(2)}, u32[]{:S(2)}) async-start(bf16[8,160,8,128]{3,2,1,0:T(8,128)(2,1)} %bitcast.4), calls=%async_computation.1 | async-start | bytes 5242880 | tf_op jit(solution)/shard_map/all_to_all | solution.py:215
  294.6 0.1 dynamic_slice.3.wave_ref
  294.7 32.2 %all-to-all-done.1.refs_0_ = bf16[8,160,8,128]{3,2,1,0:T(8,128)(2,1)S(1)} async-done(((bf16[8,160,8,128]{3,2,1,0:T(8,128)(2,1)}), bf16[8,160,8,128]{3,2,1,0:T(8,128)(2,1)S(1)}, u32[]{:S(2)}, u32[]{:S(2)}) %all-to-all-start.1) | async-done | bytes 2621472 | tf_op jit(solution)/shard_map/all_to_all | solution.py:215
  326.9 0.0 copy-start.2
  326.9 1.3 copy-done.2
  328.2 0.0 copy-start.4
  328.2 1.3 copy-done.4
  329.5 32.5 %legendre.1 = bf16[160,2,48,1280]{3,2,1,0:T(8,128)(2,1)} custom-call(s32[160]{0:T(256)S(1)} %dynamic_slice.3.wave_ref, bf16[160,128,1280]{2,1,0:T(8,128)(2,1)} %table_ref.1, bf16[8,160,8,128]{3,2,1,0:T(8,128)(2,1)S(1)} %all-to-all-done.1.refs_0_, bf16[8,160,4,128]{3,2,1,0:T(4,128)(2,1)S(1)} %copy-done.4, bf16[8,160,4,128]{3,2,1,0:T(4,128)(2,1)S(1)} %copy-done.2), custom_call_target="tpu_custom_call" | custom-call | flops 5033164800 | bytes 91750400 | tf_op jit(solution)/shard_map/legendre/pallas_call | solution.py:174
  (2 shorter events, 0.0 us)
Async XLA Ops:
  6.7 60.1 %all-to-all-start.4 = ((bf16[4,4,12,48,128]{4,3,2,1,0:T(8,128)(2,1)}), bf16[4,4,12,48,128]{4,3,2,1,0:T(8,128)(2,1)S(1)}, u32[]{:S(2)}, u32[]{:S(2)}) async-start(bf16[4,4,12,48,128]{4,3,2,1,0:T(8,128)(2,1)} %lift.5), calls=%async_computation.4 | async-start | bytes 4718592 | tf_op jit(solution)/shard_map/all_to_all | solution.py:211
  18.0 53.9 %copy-start.11 = (s32[1280]{0:T(1024)S(1)}, s32[1280]{0:T(1024)}, u32[]{:S(2)}) copy-start(s32[1280]{0:T(1024)} %param.8) | copy-start | bytes 15364
  66.9 1.4 copy-start.8
  68.3 56.9 %all-to-all-start.2 = ((bf16[4,4,12,48,128]{4,3,2,1,0:T(8,128)(2,1)}), bf16[4,4,12,48,128]{4,3,2,1,0:T(8,128)(2,1)S(1)}, u32[]{:S(2)}, u32[]{:S(2)}) async-start(bf16[4,4,12,48,128]{4,3,2,1,0:T(8,128)(2,1)} %lift.4), calls=%async_computation.2 | async-start | bytes 4718592 | tf_op jit(solution)/shard_map/all_to_all | solution.py:211
  72.0 1.7 copy-start.9
  87.0 1.1 copy-start.10
  125.2 1.4 copy-start.6
  126.7 21.9 %all-to-all-start.5 = ((bf16[8,160,4,128]{3,2,1,0:T(4,128)(2,1)}), bf16[8,160,4,128]{3,2,1,0:T(4,128)(2,1)S(1)}, u32[]{:S(2)}, u32[]{:S(2)}) async-start(bf16[8,160,4,128]{3,2,1,0:T(4,128)(2,1)} %bitcast.5), calls=%async_computation.5 | async-start | bytes 2621440 | tf_op jit(solution)/shard_map/all_to_all | solution.py:215
  137.1 2.2 copy-start
  148.6 1.1 copy-start.1
  149.8 106.9 %all-to-all-start = ((bf16[4,8,12,48,128]{4,3,2,1,0:T(8,128)(2,1)}), bf16[4,8,12,48,128]{4,3,2,1,0:T(8,128)(2,1)}, u32[]{:S(2)}, u32[]{:S(2)}) async-start(bf16[4,8,12,48,128]{4,3,2,1,0:T(8,128)(2,1)} %copy-done), calls=%async_computation | async-start | bytes 9437184 | tf_op jit(solution)/shard_map/all_to_all | solution.py:211
  154.7 1.7 copy-start.7
  256.7 32.7 %all-to-all-start.3 = ((bf16[8,160,4,128]{3,2,1,0:T(4,128)(2,1)}), bf16[8,160,4,128]{3,2,1,0:T(4,128)(2,1)S(1)}, u32[]{:S(2)}, u32[]{:S(2)}) async-start(bf16[8,160,4,128]{3,2,1,0:T(4,128)(2,1)} %bitcast.2), calls=%async_computation.3 | async-start | bytes 2621440 | tf_op jit(solution)/shard_map/all_to_all | solution.py:215
  287.9 1.5 copy-start.5
  289.4 1.1 copy-start.3
  290.4 36.5 %all-to-all-start.1 = ((bf16[8,160,8,128]{3,2,1,0:T(8,128)(2,1)}), bf16[8,160,8,128]{3,2,1,0:T(8,128)(2,1)S(1)}, u32[]{:S(2)}, u32[]{:S(2)}) async-start(bf16[8,160,8,128]{3,2,1,0:T(8,128)(2,1)} %bitcast.4), calls=%async_computation.1 | async-start | bytes 5242880 | tf_op jit(solution)/shard_map/all_to_all | solution.py:215
  326.9 1.3 copy-start.2
  328.2 1.3 copy-start.4

commit v3 on v2

--- a/solution.py
+++ b/solution.py
@@ -191,6 +191,17 @@
     )(own_waves, legendre, *pieces)
 
 
+def exchange(blocks, axis):
+    count, me = blocks.shape[0], lax.axis_index(axis)
+    out, early = blocks, None
+    for d in range(1, count):
+        block = lax.dynamic_index_in_dim(blocks, lax.rem(me + d, count), 0)
+        block = lax.ppermute(block, axis, [(i, (i + d) % count) for i in range(count)])
+        early = block if d == 1 else early
+        out = lax.dynamic_update_index_in_dim(out, block, lax.rem(me + count - d, count), 0)
+    return out, early
+
+
 def per_device(columns, vertical, row_len, wave_order, legendre):
     rows_here, blocks_here, channels, width = columns.shape
     levels = vertical.shape[0]
@@ -203,15 +214,23 @@
     scal = jnp.concatenate([row_len, first.reshape(1).astype(jnp.int32)])
     weight = jnp.kron(jnp.eye(channels // levels, dtype=vertical.dtype), vertical)
     own_waves = lax.dynamic_slice_in_dim(wave_order, lax.axis_index("band") * slots_here, slots_here)
-    pieces = []
+    pieces, received, points, points_at = [], [], None, 0
     row_at = 0
     for part in PARTS:
         rows_part = rows_here * part // sum(PARTS)
         lifted = lift(columns, weight, scal, row_at, rows_part, levs)
-        points = lax.all_to_all(lifted, "lev", split_axis=0, concat_axis=0, tiled=True)
+        if points is not None:
+            lifted, points = lax.optimization_barrier((lifted, points))
+        following, early = exchange(lifted, "lev")
+        if points is not None:
+            points, _ = lax.optimization_barrier((points, early))
+            received.append((points, points_at))
+        points, points_at = following, row_at
+        row_at += rows_part
+    received.append((points, points_at))
+    for points, row_at in received:
         coeffs = fourier(points, wave_order, scal, row_at)
-        row_at += rows_part
-        coeffs = coeffs.reshape(bands, slots_here, rows_part, coeffs.shape[-1])
+        coeffs = coeffs.reshape(bands, slots_here, *coeffs.shape[1:])
         pieces.append(lax.all_to_all(coeffs, "band", split_axis=0, concat_axis=0, tiled=True))
     return legendre_sum(own_waves, legendre, pieces, share)
 

time: 363 us -> 349 us (0.961)
  waiting for transfers between devices: 214 us -> 165 us
  starting transfers between devices: 27.6 us -> 58.7 us
  local copies, waits for them, and re-layouts: 16 us -> 20.6 us
    all_to_all x3 -> x0, waiting for transfers between devices: 172 us -> none  [per_device(): lax.all_to_all(lifted, 'lev', split_axis=0, concat_axis=0, tiled=True)]
    ppermute x0 -> x9, waiting for transfers between devices: none -> 147 us  [exchange(): lax.ppermute(block, axis, [(i, (i + d) % count) for i in range(count)])]
    ppermute x0 -> x9, starting transfers between devices: none -> 46.4 us  [exchange(): lax.ppermute(block, axis, [(i, (i + d) % count) for i in range(count)])]
    all_to_all x3, waiting for transfers between devices: 41.5 us -> 18.1 us  [per_device(): lax.all_to_all(coeffs, 'band', split_axis=0, concat_axis=0, tiled=True)]
    all_to_all x3 -> x0, starting transfers between devices: 14.9 us -> none  [per_device(): lax.all_to_all(lifted, 'lev', split_axis=0, concat_axis=0, tiled=True)]
    unnamed x24 -> x14, local copies, waits for them, and re-layouts: 15.8 us -> 5.77 us
    dynamic_slice x0 -> x6, local copies, waits for them, and re-layouts: none -> 9.44 us  [exchange(): block = lax.dynamic_index_in_dim(blocks, lax.rem(me + d, count), 0)]
    dynamic_update_slice x0 -> x6, local copies, waits for them, and re-layouts: none -> 5.14 us  [exchange(): lax.dynamic_update_index_in_dim(out, block, lax.rem(me + count - d, count...]
  transfers between devices with their start and end apart: 6 -> 12, of which waited for: 5 -> 8; matrix products, arithmetic and copies ran while one was open for 0% -> 3% of each run, Pallas kernels for 18% -> 10%
where the time goes in v3:
time: 349 us; the launch traced here: 348 us
  waiting for transfers between devices  165 us (47%)
  Pallas kernels  102 us (29%)
  starting transfers between devices  58.7 us (17%)
  local copies, waits for them, and re-layouts  20.6 us (6%)
    ppermute x9, waiting for transfers between devices, exchange(): lax.ppermute(block, axis, [(i, (i + d) % count) for i in range(count)])  147 us
    pallas_call x3, Pallas kernels, fourier(): pl.pallas_call(functools.partial(fourier_kernel, row_at=row_at, groups=gr...  53.9 us
    ppermute x9, starting transfers between devices, exchange(): lax.ppermute(block, axis, [(i, (i + d) % count) for i in range(count)])  46.4 us
    pallas_call x1, Pallas kernels, legendre_sum(): pl.pallas_call(legendre_kernel, grid_spec=pltpu.PrefetchScalarGridSpec(nu...  32.7 us
    all_to_all x3, waiting for transfers between devices, per_device(): lax.all_to_all(coeffs, 'band', split_axis=0, concat_axis=0, tiled=True)  18.1 us
    pallas_call x3, Pallas kernels, lift(): pl.pallas_call(functools.partial(lift_kernel, row_at=row_at, rows=rows),...  15.5 us
    all_to_all x3, starting transfers between devices, per_device(): lax.all_to_all(coeffs, 'band', split_axis=0, concat_axis=0, tiled=True)  12.2 us
    dynamic_slice x6, local copies, waits for them, and re-layouts, exchange(): block = lax.dynamic_index_in_dim(blocks, lax.rem(me + d, count), 0)  9.44 us
  transfers between devices with their start and end apart: 12, of which 8 were waited for; matrix products, arithmetic and copies ran while one was open for 3% of the time, Pallas kernels for 10%

profile of v3, /device:TPU:0, one launch (start us, length us, event | category | flops | bytes accessed | tf_op | source)
XLA Modules:
  0.0 348.3 jit_solution(11408303527184165198)
XLA Ops:
  0.0 0.9 broadcast_multiply_fusion
  0.9 0.2 mul.35.w_ref
  1.0 0.7 pad_add_fusion.scal_ref
  1.8 6.7 %lift.4 = bf16[4,8,12,48,128]{4,3,2,1,0:T(8,128)(2,1)S(1)} custom-call(s32[17]{0:T(128)S(1)} %pad_add_fusion.scal_ref, bf16[192,192]{1,0:T(8,128)(2,1)S(1)} %mul.35.w_ref, bf16[16,12,192,128]{3,2,1,0:T(8,128)(2,1)} %x_ref.5), custom_call_target="tpu_custom_call" | custom-call | flops 905969664 | bytes 9437184 | tf_op jit(solution)/shard_map/lift/pallas_call | solution.py:37
  8.5 0.0 copy-start
  8.5 2.2 copy-done
  10.7 0.1 constant_dynamic-slice_fusion.8
  10.7 3.1 collective-permute-start
  13.8 28.0 %collective-permute-done = bf16[1,8,12,48,128]{4,3,2,1,0:T(8,128)(2,1)S(1)} collective-permute-done((bf16[1,8,12,48,128]{4,3,2,1,0:T(8,128)(2,1)S(1)}, bf16[1,8,12,48,128]{4,3,2,1,0:T(8,128)(2,1)S(1)}, u32[]{:S(2)}, u32[]{:S(2)}) %collective-permute-start) | collective-permute-done | bytes 1179680 | tf_op jit(solution)/shard_map/ppermute | solution.py:199
  41.8 3.3 constant_dynamic-slice_fusion.6
  45.1 0.7 collective-permute-start.1
  45.8 1.3 collective-permute-start.2
  47.2 3.8 %lift.3 = bf16[4,4,12,48,128]{4,3,2,1,0:T(8,128)(2,1)S(1)} custom-call(s32[17]{0:T(128)S(1)} %pad_add_fusion.scal_ref, bf16[192,192]{1,0:T(8,128)(2,1)S(1)} %mul.35.w_ref, bf16[16,12,192,128]{3,2,1,0:T(8,128)(2,1)} %x_ref.5), custom_call_target="tpu_custom_call" | custom-call | flops 452984832 | bytes 4718592 | tf_op jit(solution)/shard_map/lift/pallas_call | solution.py:37
  51.0 46.4 %collective-permute-done.1 = bf16[1,8,12,48,128]{4,3,2,1,0:T(8,128)(2,1)S(1)} collective-permute-done((bf16[1,8,12,48,128]{4,3,2,1,0:T(8,128)(2,1)S(1)}, bf16[1,8,12,48,128]{4,3,2,1,0:T(8,128)(2,1)S(1)}, u32[]{:S(2)}, u32[]{:S(2)}) %collective-permute-start.1) | collective-permute-done | bytes 1179680 | tf_op jit(solution)/shard_map/ppermute | solution.py:199
  97.4 1.1 constant_dynamic-update-slice_fusion.7
  98.5 0.0 collective-permute-done.2
  98.5 1.1 constant_dynamic-update-slice_fusion.6.x_ref
  99.6 24.9 %collective-permute-start.3 = (bf16[1,4,12,48,128]{4,3,2,1,0:T(8,128)(2,1)S(1)}, bf16[1,4,12,48,128]{4,3,2,1,0:T(8,128)(2,1)S(1)}, u32[]{:S(2)}, u32[]{:S(2)}) collective-permute-start(bf16[1,4,12,48,128]{4,3,2,1,0:T(8,128)(2,1)S(1)} %constant_dynamic-slice_fusion.5), channel_id=1, source_target_pairs={{0,1},{1,2},{2,3},{3,0},{4,5},{5,6},{6,7},{7,4},{8,9},{9,10},{10,1... | collective-permute-start | bytes 1769480 | tf_op jit(solution)/shard_map/ppermute | solution.py:199
  124.5 16.3 %collective-permute-done.3 = bf16[1,4,12,48,128]{4,3,2,1,0:T(8,128)(2,1)S(1)} collective-permute-done((bf16[1,4,12,48,128]{4,3,2,1,0:T(8,128)(2,1)S(1)}, bf16[1,4,12,48,128]{4,3,2,1,0:T(8,128)(2,1)S(1)}, u32[]{:S(2)}, u32[]{:S(2)}) %collective-permute-start.3) | collective-permute-done | bytes 589856 | tf_op jit(solution)/shard_map/ppermute | solution.py:199
  140.8 26.4 %fourier.3 = bf16[1280,8,128]{2,1,0:T(8,128)(2,1)S(1)} custom-call(s32[17]{0:T(128)S(1)} %pad_add_fusion.scal_ref, s32[1,1280]{1,0:T(1,128)S(1)} %reshape.32.wave_ref, bf16[4,8,12,48,128]{4,3,2,1,0:T(8,128)(2,1)} %constant_dynamic-update-slice_fusion.6.x_ref), custom_call_target="tpu_custom_call" | custom-call | flops 11072962560 | bytes 12058624 | tf_op jit(solution)/shard_map/fourier/pallas_call | solution.py:130
  167.2 0.0 copy-start.3
  167.2 1.5 copy-done.3
  168.7 3.7 %all-to-all-start = ((bf16[8,160,8,128]{3,2,1,0:T(8,128)(2,1)}), bf16[8,160,8,128]{3,2,1,0:T(8,128)(2,1)S(1)}, u32[]{:S(2)}, u32[]{:S(2)}) async-start(bf16[8,160,8,128]{3,2,1,0:T(8,128)(2,1)} %bitcast.4), calls=%async_computation | async-start | bytes 5242880 | tf_op jit(solution)/shard_map/all_to_all | solution.py:234
  172.4 2.4 constant_dynamic-slice_fusion.3
  174.8 1.7 collective-permute-start.5
  176.5 5.0 %lift.5 = bf16[4,4,12,48,128]{4,3,2,1,0:T(8,128)(2,1)} custom-call(s32[17]{0:T(128)S(1)} %pad_add_fusion.scal_ref, bf16[192,192]{1,0:T(8,128)(2,1)S(1)} %mul.35.w_ref, bf16[16,12,192,128]{3,2,1,0:T(8,128)(2,1)} %x_ref.5), custom_call_target="tpu_custom_call" | custom-call | flops 452984832 | bytes 4718592 | tf_op jit(solution)/shard_map/lift/pallas_call | solution.py:37
  181.5 21.8 %collective-permute-done.4 = bf16[1,4,12,48,128]{4,3,2,1,0:T(8,128)(2,1)S(1)} collective-permute-done((bf16[1,4,12,48,128]{4,3,2,1,0:T(8,128)(2,1)S(1)}, bf16[1,4,12,48,128]{4,3,2,1,0:T(8,128)(2,1)S(1)}, u32[]{:S(2)}, u32[]{:S(2)}) %collective-permute-start.4) | collective-permute-done | bytes 589856 | tf_op jit(solution)/shard_map/ppermute | solution.py:199
  203.3 0.1 constant_dynamic-update-slice_fusion.4
  203.4 0.1 collective-permute-done.5
  203.5 0.1 constant_dynamic-update-slice_fusion.3.x_ref
  203.5 1.1 constant_dynamic-slice_fusion.2
  204.7 13.0 %collective-permute-start.6 = (bf16[1,4,12,48,128]{4,3,2,1,0:T(8,128)(2,1)S(1)}, bf16[1,4,12,48,128]{4,3,2,1,0:T(8,128)(2,1)S(1)}, u32[]{:S(2)}, u32[]{:S(2)}) collective-permute-start(bf16[1,4,12,48,128]{4,3,2,1,0:T(8,128)(2,1)S(1)} %constant_dynamic-slice_fusion.2), channel_id=1, source_target_pairs={{0,1},{1,2},{2,3},{3,0},{4,5},{5,6},{6,7},{7,4},{8,9},{9,10},{10,1... | collective-permute-start | bytes 1769480 | tf_op jit(solution)/shard_map/ppermute | solution.py:199
  217.7 15.2 %collective-permute-done.6 = bf16[1,4,12,48,128]{4,3,2,1,0:T(8,128)(2,1)S(1)} collective-permute-done((bf16[1,4,12,48,128]{4,3,2,1,0:T(8,128)(2,1)S(1)}, bf16[1,4,12,48,128]{4,3,2,1,0:T(8,128)(2,1)S(1)}, u32[]{:S(2)}, u32[]{:S(2)}) %collective-permute-start.6) | collective-permute-done | bytes 589856 | tf_op jit(solution)/shard_map/ppermute | solution.py:199
  232.8 2.6 constant_dynamic-slice_fusion
  235.4 1.7 collective-permute-start.8
  237.1 13.3 %fourier.4 = bf16[1280,4,128]{2,1,0:T(4,128)(2,1)S(1)} custom-call(s32[17]{0:T(128)S(1)} %pad_add_fusion.scal_ref, s32[1,1280]{1,0:T(1,128)S(1)} %reshape.32.wave_ref, bf16[4,4,12,48,128]{4,3,2,1,0:T(8,128)(2,1)S(1)} %constant_dynamic-update-slice_fusion.3.x_ref), custom_call_target="tpu_custom_call" | custom-call | flops 5536481280 | bytes 6029312 | tf_op jit(solution)/shard_map/fourier/pallas_call | solution.py:130
  250.4 1.0 copy-done.5
  251.5 4.3 %all-to-all-start.1 = ((bf16[8,160,4,128]{3,2,1,0:T(4,128)(2,1)}), bf16[8,160,4,128]{3,2,1,0:T(4,128)(2,1)}, u32[]{:S(2)}, u32[]{:S(2)}) async-start(bf16[8,160,4,128]{3,2,1,0:T(4,128)(2,1)} %bitcast.6), calls=%async_computation.1 | async-start | bytes 2621440 | tf_op jit(solution)/shard_map/all_to_all | solution.py:234
  255.7 19.3 %collective-permute-done.7 = bf16[1,4,12,48,128]{4,3,2,1,0:T(8,128)(2,1)} collective-permute-done((bf16[1,4,12,48,128]{4,3,2,1,0:T(8,128)(2,1)}, bf16[1,4,12,48,128]{4,3,2,1,0:T(8,128)(2,1)}, u32[]{:S(2)}, u32[]{:S(2)}) %collective-permute-start.7) | collective-permute-done | bytes 589856 | tf_op jit(solution)/shard_map/ppermute | solution.py:199
  275.1 1.9 constant_dynamic-update-slice_fusion.1
  277.0 0.9 constant_dynamic-update-slice_fusion.x_ref
  277.9 14.2 %fourier.5 = bf16[1280,4,128]{2,1,0:T(4,128)(2,1)S(1)} custom-call(s32[17]{0:T(128)S(1)} %pad_add_fusion.scal_ref, s32[1,1280]{1,0:T(1,128)S(1)} %reshape.32.wave_ref, bf16[4,4,12,48,128]{4,3,2,1,0:T(8,128)(2,1)} %constant_dynamic-update-slice_fusion.x_ref), custom_call_target="tpu_custom_call" | custom-call | flops 5536481280 | bytes 6029312 | tf_op jit(solution)/shard_map/fourier/pallas_call | solution.py:130
  292.0 0.0 copy-start.4
  292.0 1.0 copy-done.4
  293.1 4.3 %all-to-all-start.2 = ((bf16[8,160,4,128]{3,2,1,0:T(4,128)(2,1)}), bf16[8,160,4,128]{3,2,1,0:T(4,128)(2,1)}, u32[]{:S(2)}, u32[]{:S(2)}) async-start(bf16[8,160,4,128]{3,2,1,0:T(4,128)(2,1)} %bitcast.5), calls=%async_computation.2 | async-start | bytes 2621440 | tf_op jit(solution)/shard_map/all_to_all | solution.py:234
  297.4 0.1 dynamic_slice.32.wave_ref
  297.5 18.1 %all-to-all-done.2.refs_2_ = bf16[8,160,4,128]{3,2,1,0:T(4,128)(2,1)} async-done(((bf16[8,160,4,128]{3,2,1,0:T(4,128)(2,1)}), bf16[8,160,4,128]{3,2,1,0:T(4,128)(2,1)}, u32[]{:S(2)}, u32[]{:S(2)}) %all-to-all-start.2) | async-done | bytes 1310752 | tf_op jit(solution)/shard_map/all_to_all | solution.py:234
  315.6 32.7 %legendre.1 = bf16[160,2,48,1280]{3,2,1,0:T(8,128)(2,1)} custom-call(s32[160]{0:T(256)S(1)} %dynamic_slice.32.wave_ref, bf16[160,128,1280]{2,1,0:T(8,128)(2,1)} %table_ref.1, bf16[8,160,8,128]{3,2,1,0:T(8,128)(2,1)S(1)} %all-to-all-done.refs_0_, bf16[8,160,4,128]{3,2,1,0:T(4,128)(2,1)} %all-to-all-done.1.refs_1_, bf16[8,160,4,128]{3,2,1,0:T(4,128)(2,1)} %all-to-all-done.2.refs_2_), custom_call_target="tpu_custom_call" | custom-call | flops 5033164800 | bytes 91750400 | tf_op jit(solution)/shard_map/legendre/pallas_call | solution.py:174
  (15 shorter events, 0.1 us)
Async XLA Ops:
  8.5 2.2 copy-start
  10.7 31.1 %collective-permute-start = (bf16[1,8,12,48,128]{4,3,2,1,0:T(8,128)(2,1)S(1)}, bf16[1,8,12,48,128]{4,3,2,1,0:T(8,128)(2,1)S(1)}, u32[]{:S(2)}, u32[]{:S(2)}) collective-permute-start(bf16[1,8,12,48,128]{4,3,2,1,0:T(8,128)(2,1)S(1)} %constant_dynamic-slice_fusion.8), channel_id=1, source_target_pairs={{0,1},{1,2},{2,3},{3,0},{4,5},{5,6},{6,7},{7,4},{8,9},{9,10},{10,1... | collective-permute-start | bytes 3538952 | tf_op jit(solution)/shard_map/ppermute | solution.py:199
  45.1 52.3 %collective-permute-start.1 = (bf16[1,8,12,48,128]{4,3,2,1,0:T(8,128)(2,1)S(1)}, bf16[1,8,12,48,128]{4,3,2,1,0:T(8,128)(2,1)S(1)}, u32[]{:S(2)}, u32[]{:S(2)}) collective-permute-start(bf16[1,8,12,48,128]{4,3,2,1,0:T(8,128)(2,1)S(1)} %get-tuple-element.18), channel_id=1, source_target_pairs={{0,2},{1,3},{2,0},{3,1},{4,6},{5,7},{6,4},{7,5},{8,10},{9,11},{10,... | collective-permute-start | bytes 3538952 | tf_op jit(solution)/shard_map/ppermute | solution.py:199
  45.8 52.7 %collective-permute-start.2 = (bf16[1,8,12,48,128]{4,3,2,1,0:T(8,128)(2,1)S(1)}, bf16[1,8,12,48,128]{4,3,2,1,0:T(8,128)(2,1)S(1)}, u32[]{:S(2)}, u32[]{:S(2)}) collective-permute-start(bf16[1,8,12,48,128]{4,3,2,1,0:T(8,128)(2,1)S(1)} %get-tuple-element.17), channel_id=1, source_target_pairs={{0,3},{1,0},{2,1},{3,2},{4,7},{5,4},{6,5},{7,6},{8,11},{9,8},{10,9... | collective-permute-start | bytes 3538952 | tf_op jit(solution)/shard_map/ppermute | solution.py:199
  51.0 48.6 %copy-start.1 = (bf16[4,4,12,48,128]{4,3,2,1,0:T(8,128)(2,1)}, bf16[4,4,12,48,128]{4,3,2,1,0:T(8,128)(2,1)S(1)}, u32[]{:S(2)}) copy-start(bf16[4,4,12,48,128]{4,3,2,1,0:T(8,128)(2,1)S(1)} %lift.3) | copy-start | bytes 7077892
  98.5 26.0 %copy-start.6 = (s32[1280]{0:T(1024)S(1)}, s32[1280]{0:T(1024)}, u32[]{:S(2)}) copy-start(s32[1280]{0:T(1024)} %param.8) | copy-start | bytes 15364
  99.6 41.2 %collective-permute-start.3 = (bf16[1,4,12,48,128]{4,3,2,1,0:T(8,128)(2,1)S(1)}, bf16[1,4,12,48,128]{4,3,2,1,0:T(8,128)(2,1)S(1)}, u32[]{:S(2)}, u32[]{:S(2)}) collective-permute-start(bf16[1,4,12,48,128]{4,3,2,1,0:T(8,128)(2,1)S(1)} %constant_dynamic-slice_fusion.5), channel_id=1, source_target_pairs={{0,1},{1,2},{2,3},{3,0},{4,5},{5,6},{6,7},{7,4},{8,9},{9,10},{10,1... | collective-permute-start | bytes 1769480 | tf_op jit(solution)/shard_map/ppermute | solution.py:199
  167.2 1.5 copy-start.3
  168.7 82.7 %all-to-all-start = ((bf16[8,160,8,128]{3,2,1,0:T(8,128)(2,1)}), bf16[8,160,8,128]{3,2,1,0:T(8,128)(2,1)S(1)}, u32[]{:S(2)}, u32[]{:S(2)}) async-start(bf16[8,160,8,128]{3,2,1,0:T(8,128)(2,1)} %bitcast.4), calls=%async_computation | async-start | bytes 5242880 | tf_op jit(solution)/shard_map/all_to_all | solution.py:234
  174.8 28.5 %collective-permute-start.4 = (bf16[1,4,12,48,128]{4,3,2,1,0:T(8,128)(2,1)S(1)}, bf16[1,4,12,48,128]{4,3,2,1,0:T(8,128)(2,1)S(1)}, u32[]{:S(2)}, u32[]{:S(2)}) collective-permute-start(bf16[1,4,12,48,128]{4,3,2,1,0:T(8,128)(2,1)S(1)} %get-tuple-element.24), channel_id=1, source_target_pairs={{0,2},{1,3},{2,0},{3,1},{4,6},{5,7},{6,4},{7,5},{8,10},{9,11},{10,... | collective-permute-start | bytes 1769480 | tf_op jit(solution)/shard_map/ppermute | solution.py:199
  174.8 28.5 %copy-start.2 = (bf16[4,4,12,48,128]{4,3,2,1,0:T(8,128)(2,1)S(1)}, bf16[4,4,12,48,128]{4,3,2,1,0:T(8,128)(2,1)}, u32[]{:S(2)}) copy-start(bf16[4,4,12,48,128]{4,3,2,1,0:T(8,128)(2,1)} %get-tuple-element.25) | copy-start | bytes 7077892
  174.8 28.6 %collective-permute-start.5 = (bf16[1,4,12,48,128]{4,3,2,1,0:T(8,128)(2,1)S(1)}, bf16[1,4,12,48,128]{4,3,2,1,0:T(8,128)(2,1)S(1)}, u32[]{:S(2)}, u32[]{:S(2)}) collective-permute-start(bf16[1,4,12,48,128]{4,3,2,1,0:T(8,128)(2,1)S(1)} %get-tuple-element.23), channel_id=1, source_target_pairs={{0,3},{1,0},{2,1},{3,2},{4,7},{5,4},{6,5},{7,6},{8,11},{9,8},{10,9... | collective-permute-start | bytes 1769480 | tf_op jit(solution)/shard_map/ppermute | solution.py:199
  204.7 28.2 %collective-permute-start.6 = (bf16[1,4,12,48,128]{4,3,2,1,0:T(8,128)(2,1)S(1)}, bf16[1,4,12,48,128]{4,3,2,1,0:T(8,128)(2,1)S(1)}, u32[]{:S(2)}, u32[]{:S(2)}) collective-permute-start(bf16[1,4,12,48,128]{4,3,2,1,0:T(8,128)(2,1)S(1)} %constant_dynamic-slice_fusion.2), channel_id=1, source_target_pairs={{0,1},{1,2},{2,3},{3,0},{4,5},{5,6},{6,7},{7,4},{8,9},{9,10},{10,1... | collective-permute-start | bytes 1769480 | tf_op jit(solution)/shard_map/ppermute | solution.py:199
  235.4 41.6 %collective-permute-start.8 = (bf16[1,4,12,48,128]{4,3,2,1,0:T(8,128)(2,1)}, bf16[1,4,12,48,128]{4,3,2,1,0:T(8,128)(2,1)S(1)}, u32[]{:S(2)}, u32[]{:S(2)}) collective-permute-start(bf16[1,4,12,48,128]{4,3,2,1,0:T(8,128)(2,1)} %get-tuple-element.20), channel_id=1, source_target_pairs={{0,3},{1,0},{2,1},{3,2},{4,7},{5,4},{6,5},{7,6},{8,11},{9,8},{10,9... | collective-permute-start | bytes 1769480 | tf_op jit(solution)/shard_map/ppermute | solution.py:199
  237.1 38.0 %collective-permute-start.7 = (bf16[1,4,12,48,128]{4,3,2,1,0:T(8,128)(2,1)}, bf16[1,4,12,48,128]{4,3,2,1,0:T(8,128)(2,1)}, u32[]{:S(2)}, u32[]{:S(2)}) collective-permute-start(bf16[1,4,12,48,128]{4,3,2,1,0:T(8,128)(2,1)} %get-tuple-element.21), channel_id=1, source_target_pairs={{0,2},{1,3},{2,0},{3,1},{4,6},{5,7},{6,4},{7,5},{8,10},{9,11},{10,... | collective-permute-start | bytes 1769480 | tf_op jit(solution)/shard_map/ppermute | solution.py:199
  250.4 1.0 copy-start.5
  251.5 41.6 %all-to-all-start.1 = ((bf16[8,160,4,128]{3,2,1,0:T(4,128)(2,1)}), bf16[8,160,4,128]{3,2,1,0:T(4,128)(2,1)}, u32[]{:S(2)}, u32[]{:S(2)}) async-start(bf16[8,160,4,128]{3,2,1,0:T(4,128)(2,1)} %bitcast.6), calls=%async_computation.1 | async-start | bytes 2621440 | tf_op jit(solution)/shard_map/all_to_all | solution.py:234
  292.0 1.1 copy-start.4
  293.1 22.5 %all-to-all-start.2 = ((bf16[8,160,4,128]{3,2,1,0:T(4,128)(2,1)}), bf16[8,160,4,128]{3,2,1,0:T(4,128)(2,1)}, u32[]{:S(2)}, u32[]{:S(2)}) async-start(bf16[8,160,4,128]{3,2,1,0:T(4,128)(2,1)} %bitcast.5), calls=%async_computation.2 | async-start | bytes 2621440 | tf_op jit(solution)/shard_map/all_to_all | solution.py:234
